TPU v7x, 32 devices: a whole 2x2x4 slice. The times are simulated.
32 devices in a mesh: lead: 8 (over z, x), sub: 4 (over y, core).
Axes of the slice: x: 2, y: 2, z: 4, core: 2. Of those that a mesh axis runs over, the one named last changes fastest.
Arguments:
- state: float32 [67108864], P(('lead', 'sub')), may hold values from 0.135 to 67, as said below
- couplings: float32 [2, 16], replicated, may hold values from 0.25 to 16, as said below
Outputs:
- evolved: float32 [67108864], P(('lead', 'sub'))
- log_growth: float32 [], replicated
Inputs may be any that keep to these rules, and one draw needn't show every extreme that they name: `state`: every entry is positive. `couplings`: row 0 lies between 8 and 16, row 1 between 0.25 and 0.5.
All inputs are finite; a program needn't handle non-finite values.
Results may differ from a plain program's by a relative error of at most 0.0003.
Values sent between devices are 32-bit elements; how exact they have to be, the bound alone decides.
A program may use at most 128 MiB of HBM per device.

v0:
```python
import jax
import jax.numpy as jnp
from jax import lax
from jax.sharding import PartitionSpec as P

BLOCK = 4
WINDOWS = 2


def block_kernel(vertical, horizontal, spread):
    position = jnp.arange(spread, dtype=jnp.int32)
    digits = [position // 4 ** (BLOCK - 1 - level) % 4 for level in range(BLOCK)]
    kernel = jnp.ones((spread, spread), jnp.float32)
    for level in range(BLOCK):
        same_spin = (digits[level][:, None] == digits[level][None, :]).astype(jnp.float32)
        kernel = kernel * (1.0 + vertical[level] * same_spin)
    for level in range(1, BLOCK):
        chained = (digits[level - 1] == digits[level]).astype(jnp.float32)
        kernel = kernel * (1.0 + horizontal[level] * chained)[None, :]
    labels = jnp.arange(4, dtype=jnp.int32)
    first_bond = 1.0 + horizontal[0] * (labels[:, None] == labels[None, :]).astype(jnp.float32)
    return (kernel, first_bond)


def multiply(matrix, kernel):
    return lax.dot_general(
        matrix,
        kernel,
        (((0,), (0,)), ((), ())),
        precision=lax.Precision.HIGHEST,
        preferred_element_type=jnp.float32,
    )


def bond_first(result, first_bond, spread):
    bonded = result.reshape(-1, 4, 4, spread // 4) * first_bond[None, :, :, None]
    return bonded.reshape(-1)


def contract_first(received, kernel, spread):
    item_count = received.shape[-1]
    return multiply(received.reshape(spread, -1, item_count), kernel)


def regroup(current, block_depth, kernel, first_bond, lead_count, sub_count, spread):
    devices = lead_count * sub_count
    span_rows = spread**block_depth
    low_rows = span_rows // devices
    rest_cols = current.shape[0] // span_rows
    shaped = current.reshape(1, low_rows, devices, rest_cols)
    result = contract_first(
        lax.all_to_all(shaped, ("lead", "sub"), split_axis=2, concat_axis=0, tiled=True),
        kernel,
        spread,
    )
    return bond_first(result, first_bond, spread)


def local_block(current, kernel, first_bond, spread):
    result = multiply(current.reshape(spread, -1), kernel)
    return bond_first(result, first_bond, spread)


def shards(state, couplings):
    lead_count = lax.axis_size("lead")
    sub_count = lax.axis_size("sub")
    devices = lead_count * sub_count
    spread = 4**BLOCK
    whole_count = state.shape[0] * devices
    period_blocks = 2
    current = state
    growth = jnp.zeros((), jnp.float32)
    for window in range(WINDOWS):
        for half_step in range(2):
            first_site = (2 * window + half_step) * BLOCK
            kernel, first_bond = block_kernel(
                couplings[0, first_site : first_site + BLOCK],
                couplings[1, first_site : first_site + BLOCK],
                spread,
            )
            if half_step % period_blocks == 0:
                current = regroup(
                    current, period_blocks, kernel, first_bond, lead_count, sub_count, spread
                )
            else:
                current = local_block(current, kernel, first_bond, spread)
        grand_total = lax.psum(jnp.sum(current), ("lead", "sub"))
        mean_value = grand_total / whole_count
        current = current / mean_value
        growth = growth + jnp.log(mean_value)
    return (current, growth)


def solution(mesh):
    in_specs = (P(("lead", "sub")), P())
    out_specs = (P(("lead", "sub")), P())
    return jax.shard_map(shards, mesh=mesh, in_specs=in_specs, out_specs=out_specs, check_vma=False)
```

profile of v0, /device:TPU:0, one launch (start us, length us, event | category | flops | bytes accessed | tf_op | source)
XLA Modules:
  0.0 779.1 jit_solution(12016127203400008424)
XLA Ops:
  0.6 20.6 %reshape.637 = f32[1,2048,32,32]{3,2,1,0:T(8,128)} reshape(f32[2097152]{0:T(1024)} %param.2) | data formatting | bytes 16777216 | tf_op jit(solution)/shard_map/reshape | solution.py:50
  21.3 21.7 %copy.15 = f32[1,2048,32,32]{1,3,0,2:T(8,128)} copy(f32[1,2048,32,32]{3,2,1,0:T(8,128)} %reshape.637) | data formatting | bytes 16777216 | tf_op jit(solution)/shard_map/reshape | solution.py:50
  43.0 0.0 copy-start
  43.0 7.4 all-to-all-start
  50.4 0.0 copy-done
  50.4 0.7 fusion.171
  51.1 0.6 select_add_fusion.12
  51.8 6.3 mul.492
  58.1 16.7 %mul.493 = f32[256,8192]{1,0:T(8,128)} reshape(f32[2048,4,4,64]{3,2,1,0:T(4,128)} %mul.492) | data formatting | bytes 16777216 | tf_op jit(solution)/shard_map/mul | solution.py:36
  74.8 0.6 fusion.154
  75.4 0.7 fusion.170
  76.1 0.6 select_add_fusion.8
  76.8 0.6 select_add_fusion.11
  77.3 1.3 fusion.152
  78.7 1.2 select_add_fusion.9
  79.9 155.8 %all-to-all-done = f32[1,2048,32,32]{1,3,0,2:T(8,128)} async-done(((f32[1,2048,32,32]{1,3,0,2:T(8,128)}), f32[1,2048,32,32]{1,3,0,2:T(8,128)}, u32[]{:S(2)}, u32[]{:S(2)}) %all-to-all-start) | async-done | bytes 8388640 | tf_op jit(solution)/shard_map/all_to_all | solution.py:52
  235.7 11.6 %copy.16 = f32[32,1,2048,1,32]{2,0,4,3,1:T(8,128)} copy(f32[32,1,2048,1,32]{2,4,0,3,1:T(8,128)} %bitcast.9) | data formatting | bytes 16777216 | tf_op jit(solution)/shard_map/all_to_all | solution.py:52
  247.3 9.3 %reshape.638 = f32[256,256,32]{1,0,2:T(8,128)} reshape(f32[32,1,2048,1,32]{2,0,4,3,1:T(8,128)} %copy.16) | data formatting | bytes 16777216 | tf_op jit(solution)/shard_map/reshape | solution.py:42
  256.6 14.6 %fusion.54 = f32[256,256,32]{1,0,2:T(8,128)} fusion(f32[256,256,32]{1,0,2:T(8,128)} %reshape.638, f32[256]{0:T(256)S(1)} %fusion.154, f32[256]{0:T(256)S(1)} %get-tuple-element.43, f32[256]{0:T(256)S(1)} %get-tuple-element.42, f32[]{:T(128)} %bitcast.3, s32[256]{0:T(256)S(1)} %get-tuple-element.38, f32[]{:T(128)} %bitcast.2, s32[256]{0:T(256)S(1)} %get-tuple-element.39, ...), kind=kOutput, calls=%fused_computation.57 | convolution fusion | flops 6443630592 | bytes 16784400 | tf_op jit(solution)/shard_map/dot_general | solution.py:26
  271.2 9.1 %copy.17 = f32[256,8192]{1,0:T(8,128)} copy(f32[256,8192]{0,1:T(8,128)} %bitcast.81) | data formatting | bytes 16777216 | tf_op jit(solution)/shard_map/reshape | solution.py:36
  280.3 10.4 %multiply_bitcast_fusion = f32[8192,256]{0,1:T(8,128)} fusion(f32[256,8192]{1,0:T(8,128)} %copy.17, f32[256,8192]{1,0:T(8,128)} %mul.493), kind=kLoop, calls=%fused_computation.6 | loop fusion | flops 2097152 | bytes 25165824 | tf_op jit(solution)/shard_map/dot_general | solution.py:26
  290.8 9.0 %copy.18 = f32[8192,256]{1,0:T(8,128)} copy(f32[8192,256]{0,1:T(8,128)} %multiply_bitcast_fusion) | data formatting | bytes 16777216 | tf_op jit(solution)/shard_map/dot_general | solution.py:26
  299.8 9.7 %dot_general.29 = f32[2048,4,256]{2,1,0:T(4,128)} reshape(f32[8192,256]{1,0:T(8,128)} %copy.18) | data formatting | bytes 16777216 | tf_op jit(solution)/shard_map/dot_general | solution.py:26
  309.5 17.5 %multiply_reduce_fusion.1 = (f32[]{:T(128)}, f32[2048,4,4,64]{0,3,2,1:T(8,128)}) fusion(f32[4,4]{1,0:T(4,128)S(1)} %select_add_fusion.8, f32[4,64]{1,0:T(4,128)S(1)} %get-tuple-element.48, f32[4,64]{1,0:T(4,128)S(1)} %get-tuple-element.49, f32[4,64]{1,0:T(4,128)S(1)} %select_add_fusion.11, f32[]{:T(128)} %bitcast.18, s32[4,64]{1,0:T(4,128)S(1)} %get-tuple-element.44, ...), kind=kOutput, calls=%fused_computation.10 | convolution fusion | flops 6447824896 | bytes 16788564 | tf_op jit(solution)/shard_map/dot_general | solution.py:26
  327.0 41.6 %psum.14 = f32[]{:T(128)} all-reduce(f32[]{:T(128)} %get-tuple-element.34), channel_id=1, replica_groups=mesh['lead'=8,'sub'=4] {'lead','sub'}, use_global_device_ids=true, to_apply=%region_1.2 | all-reduce | flops 1 | bytes 8 | tf_op jit(solution)/shard_map/psum | solution.py:87
  369.2 8.7 %multiply_divide_fusion.1 = f32[2048,4,4,64]{0,3,2,1:T(8,128)} fusion(f32[2048,4,4,64]{0,3,2,1:T(8,128)} %get-tuple-element.35, f32[]{:T(128)S(6)} %div.165, f32[4,4]{1,0:T(4,128)S(1)} %select_add_fusion.8), kind=kLoop, calls=%fused_computation.9 | loop fusion | flops 4194304 | bytes 16777284 | tf_op jit(solution)/shard_map/div | solution.py:89
  378.0 5.8 all-to-all-start.1
  383.7 0.6 select_add_fusion.4
  384.3 0.6 select_add_fusion.7
  384.9 0.7 select_add_fusion
  385.6 0.6 select_add_fusion.3
  386.2 1.3 select_add_fusion.5
  387.5 1.2 select_add_fusion.1
  388.8 180.2 %all-to-all-done.1 = f32[1,2048,32,32]{1,3,0,2:T(8,128)} async-done(((f32[1,2048,32,32]{1,3,0,2:T(8,128)}), f32[1,2048,32,32]{1,3,0,2:T(8,128)}, u32[]{:S(2)}, u32[]{:S(2)}) %all-to-all-start.1) | async-done | bytes 8388640 | tf_op jit(solution)/shard_map/all_to_all | solution.py:52
  569.0 11.6 %copy.21 = f32[32,1,2048,1,32]{2,0,4,3,1:T(8,128)} copy(f32[32,1,2048,1,32]{2,4,0,3,1:T(8,128)} %bitcast.27) | data formatting | bytes 16777216 | tf_op jit(solution)/shard_map/all_to_all | solution.py:52
  580.6 9.3 %reshape.640 = f32[256,256,32]{1,0,2:T(8,128)} reshape(f32[32,1,2048,1,32]{2,0,4,3,1:T(8,128)} %copy.21) | data formatting | bytes 16777216 | tf_op jit(solution)/shard_map/reshape | solution.py:42
  589.9 10.2 %copy.22 = f32[256,32,256]{2,1,0:T(8,128)} copy(f32[256,32,256]{0,2,1:T(8,128)} %bitcast.82) | data formatting | bytes 16777216 | tf_op jit(solution)/shard_map/dot_general | solution.py:26
  600.1 9.8 %dot_general.32 = f32[2048,4,256]{2,1,0:T(4,128)} reshape(f32[256,32,256]{2,1,0:T(8,128)} %copy.22) | data formatting | bytes 16777216 | tf_op jit(solution)/shard_map/dot_general | solution.py:26
  609.9 16.5 %fusion.6 = f32[2048,4,4,64]{0,3,2,1:T(8,128)} fusion(f32[2048,4,256,1]{2,1,0,3:T(4,128)} %bitcast.80, f32[4,4]{1,0:T(4,128)S(1)} %select_add_fusion.4, f32[4,64]{1,0:T(4,128)S(1)} %get-tuple-element.50, f32[4,64]{1,0:T(4,128)S(1)} %get-tuple-element.51, f32[4,64]{1,0:T(4,128)S(1)} %select_add_fusion.7, f32[]{:T(128)} %bitcast.33, f32[]{:T(128)} %bitcast.32, ...), kind=kOutput, calls=%fused_computation.11 | convolution fusion | flops 6445727744 | bytes 16788560 | tf_op jit(solution)/shard_map/dot_general | solution.py:26
  626.4 16.1 %copy.24 = f32[2048,4,4,64]{3,2,1,0:T(4,128)} copy(f32[2048,4,4,64]{0,3,2,1:T(8,128)} %fusion.6) | data formatting | bytes 16777216 | tf_op jit(solution)/shard_map/mul | solution.py:36
  642.4 16.8 %reshape_reshape.4 = f32[256,8192]{1,0:T(8,128)} reshape(f32[2048,4,4,64]{3,2,1,0:T(4,128)} %copy.24) | data formatting | bytes 16777216 | tf_op jit(solution)/shard_map/reshape;reshape | solution.py:60
  659.3 9.0 %copy.25 = f32[8192,256]{1,0:T(8,128)} copy(f32[8192,256]{0,1:T(8,128)} %bitcast.76) | data formatting | bytes 16777216 | tf_op jit(solution)/shard_map/dot_general | solution.py:26
  668.3 9.7 %dot_general.35 = f32[2048,4,256]{2,1,0:T(4,128)} reshape(f32[8192,256]{1,0:T(8,128)} %copy.25) | data formatting | bytes 16777216 | tf_op jit(solution)/shard_map/dot_general | solution.py:26
  678.0 17.3 %multiply_reduce_fusion = (f32[]{:T(128)}, f32[2048,4,4,64]{0,3,2,1:T(8,128)}) fusion(f32[4,4]{1,0:T(4,128)S(1)} %select_add_fusion, f32[4,64]{1,0:T(4,128)S(1)} %get-tuple-element.52, f32[4,64]{1,0:T(4,128)S(1)} %get-tuple-element.53, f32[4,64]{1,0:T(4,128)S(1)} %select_add_fusion.3, f32[]{:T(128)} %bitcast.44, f32[]{:T(128)} %bitcast.43, f32[]{:T(128)} %bitcast.42, ...), kind=kOutput, calls=%fused_computation.8 | convolution fusion | flops 6447824896 | bytes 16788564 | tf_op jit(solution)/shard_map/dot_general | solution.py:26
  695.4 41.5 %psum.15 = f32[]{:T(128)} all-reduce(f32[]{:T(128)} %get-tuple-element.36), channel_id=1, replica_groups=mesh['lead'=8,'sub'=4] {'lead','sub'}, use_global_device_ids=true, to_apply=%region_3.4 | all-reduce | flops 1 | bytes 8 | tf_op jit(solution)/shard_map/psum | solution.py:87
  737.6 8.7 %multiply_divide_fusion = f32[2048,4,4,64]{0,3,2,1:T(8,128)} fusion(f32[2048,4,4,64]{0,3,2,1:T(8,128)} %get-tuple-element.37, f32[]{:T(128)S(6)} %div.169, f32[4,4]{1,0:T(4,128)S(1)} %select_add_fusion), kind=kLoop, calls=%fused_computation.7 | loop fusion | flops 4194304 | bytes 16777284 | tf_op jit(solution)/shard_map/div | solution.py:89
  746.4 16.1 %copy.27 = f32[2048,4,4,64]{3,2,1,0:T(4,128)} copy(f32[2048,4,4,64]{0,3,2,1:T(8,128)} %multiply_divide_fusion) | data formatting | bytes 16777216 | tf_op jit(solution)/shard_map/div | solution.py:89
  762.4 15.4 %div.172 = f32[2097152]{0:T(1024)} reshape(f32[2048,4,4,64]{3,2,1,0:T(4,128)} %copy.27) | data formatting | bytes 16777216 | tf_op jit(solution)/shard_map/div | solution.py:89
  (4 shorter events, 0.0 us)
Async XLA Ops:
  43.0 7.4 copy-start
  43.0 192.7 %all-to-all-start = ((f32[1,2048,32,32]{1,3,0,2:T(8,128)}), f32[1,2048,32,32]{1,3,0,2:T(8,128)}, u32[]{:S(2)}, u32[]{:S(2)}) async-start(f32[1,2048,32,32]{1,3,0,2:T(8,128)} %copy.15), calls=%async_computation | async-start | bytes 16777216 | tf_op jit(solution)/shard_map/all_to_all | solution.py:52
  378.0 191.0 %all-to-all-start.1 = ((f32[1,2048,32,32]{1,3,0,2:T(8,128)}), f32[1,2048,32,32]{1,3,0,2:T(8,128)}, u32[]{:S(2)}, u32[]{:S(2)}) async-start(f32[1,2048,32,32]{1,3,0,2:T(8,128)} %bitcast.77), calls=%async_computation.1 | async-start | bytes 16777216 | tf_op jit(solution)/shard_map/all_to_all | solution.py:52
where the time goes:
time: 794 us; the launch traced here: 779 us
  waiting for transfers between devices  336 us (42%)
  local copies, waits for them, and re-layouts  240 us (30%)
  blocking collectives  83.1 us (10%)
  matrix products  65.9 us (8%)
  other arithmetic  37.9 us (5%)
  starting transfers between devices  13.2 us (2%)
    all_to_all x2, waiting for transfers between devices, regroup(): lax.all_to_all(shaped, ('lead', 'sub'), split_axis=2, concat_axis=0, tile...  336 us
    psum x2, blocking collectives, shards(): grand_total = lax.psum(jnp.sum(current), ('lead', 'sub'))  83.1 us
    dot_general x4, matrix products, multiply(): lax.dot_general(matrix, kernel, (((0,), (0,)), ((), ())), precision=lax.P...  65.9 us
    dot_general x6, local copies, waits for them, and re-layouts, multiply(): lax.dot_general(matrix, kernel, (((0,), (0,)), ((), ())), precision=lax.P...  57.5 us
    reshape x2, local copies, waits for them, and re-layouts, regroup(): shaped = current.reshape(1, low_rows, devices, rest_cols)  42.4 us
    mul x3, local copies, waits for them, and re-layouts, bond_first(): result.reshape(-1, 4, 4, spread // 4) * first_bond[None, :, :, None]  39 us
    div x2, local copies, waits for them, and re-layouts, shards(): current = current / mean_value  31.4 us
    all_to_all x2, local copies, waits for them, and re-layouts, regroup(): lax.all_to_all(shaped, ('lead', 'sub'), split_axis=2, concat_axis=0, tile...  23.3 us
  transfers between devices with their start and end apart: 2, of which 2 were waited for; matrix products, arithmetic and copies ran while one was open for 4% of the time, Pallas kernels for 0%

commit v1 on v0

--- a/solution.py
+++ b/solution.py
@@ -1,6 +1,8 @@
 import jax
 import jax.numpy as jnp
 from jax import lax
+from jax.experimental import pallas as pl
+from jax.experimental.pallas import tpu as pltpu
 from jax.sharding import PartitionSpec as P
 
 BLOCK = 4
@@ -91,7 +93,292 @@
     return (current, growth)
 
 
+MESH = pl.DeviceIdType.MESH
+DEVICES = 32
+CHUNKS = 4
+
+
+def split(value):
+    high = value.astype(jnp.bfloat16)
+    return high, (value - high.astype(jnp.float32)).astype(jnp.bfloat16)
+
+
+def dot3(left, right, dims):
+    (lh, ll), (rh, rl) = left, right
+    dot = lambda a, b: lax.dot_general(a, b, (dims, ((), ())), preferred_element_type=jnp.float32)
+    return dot(lh, rh) + (dot(lh, rl) + dot(ll, rh))
+
+
+def digit(index, place):
+    return (index // 4**place) % 4
+
+
+def partner(me, step):
+    other = 0
+    for bit in range(5):
+        a, b = (me // 2**bit) % 2, (step // 2**bit) % 2
+        other = other + (a + b - 2 * a * b) * 2**bit
+    return other
+
+
+def place_of(device):
+    return (device // 4, device % 4)
+
+
+def exchange_kernel(
+    coup, x_hbm, u_hbm, total_ref,
+    xin, sbuf, rbuf, stage, l_hi, l_lo, a_hi, a_lo, k_hi, k_lo, factor, part, gathered,
+    in_sem, out_sem, own_sem, send_sem, recv_sem, sum_send, sum_recv,
+):
+    me = lax.axis_index("lead") * 4 + lax.axis_index("sub")
+    d3, d4, d5_high = me // 8, (me // 2) % 4, me % 2
+
+    def v(site):
+        return coup[0, site]
+
+    def h(site):
+        return coup[1, site]
+
+    loads = [
+        pltpu.make_async_copy(x_hbm.at[half], xin.at[half], in_sem.at[half]) for half in range(2)
+    ]
+    for load in loads:
+        load.start()
+
+    barrier = pltpu.get_barrier_semaphore()
+
+    @pl.loop(1, DEVICES)
+    def _(step):
+        pl.semaphore_signal(
+            barrier, inc=1, device_id=place_of(partner(me, step)), device_id_type=MESH
+        )
+
+    pl.semaphore_wait(barrier, DEVICES - 1)
+
+    def bond(site, one, other):
+        return jnp.where(one == other, 1.0 + h(site), 1.0)
+
+    def hop(site, one, other):
+        return jnp.where(one == other, 1.0 + v(site), 1.0)
+
+    rows = lax.broadcasted_iota(jnp.int32, (256, 256), 0)
+    cols = lax.broadcasted_iota(jnp.int32, (256, 256), 1)
+    a_mat = hop(5, digit(rows, 3), digit(cols, 3)) * hop(6, digit(rows, 2), digit(cols, 2))
+    a_mat = a_mat * hop(7, digit(rows, 1), digit(cols, 1)) * hop(8, digit(rows, 0), digit(cols, 0))
+    a_hi[...], a_lo[...] = split(a_mat)
+    l_mat = hop(9, digit(rows, 3), digit(cols, 3)) * hop(10, digit(rows, 1), digit(cols, 2))
+    l_mat = l_mat * hop(11, digit(rows, 0), digit(cols, 1))
+    l_mat = jnp.where(digit(rows, 2) == digit(cols, 0), l_mat, 0.0)
+    l_hi[...], l_lo[...] = split(l_mat)
+
+    def copy_to(chunk, step):
+        other = partner(me, step)
+        return pltpu.make_async_remote_copy(
+            src_ref=sbuf.at[chunk, other],
+            dst_ref=rbuf.at[chunk, pl.ds(pl.multiple_of(me * 128, 128), 128)],
+            send_sem=send_sem.at[chunk, step],
+            recv_sem=recv_sem.at[chunk, step],
+            device_id=place_of(other),
+            device_id_type=MESH,
+        )
+
+    for load in loads:
+        load.wait()
+
+    for half in range(2):
+
+        @pl.loop(0, 512, step=8)
+        def _(row):
+            where = pl.ds(pl.multiple_of(row, 8), 8)
+            values = [xin[half, block, where, :] for block in range(16)]
+            for site, stride in ((3, 4), (4, 1)):
+                fresh = list(values)
+                for first in range(16):
+                    if (first // stride) % 4 == 0:
+                        group = [first + stride * spin for spin in range(4)]
+                        total = (values[group[0]] + values[group[1]]) + (
+                            values[group[2]] + values[group[3]]
+                        )
+                        for member in group:
+                            fresh[member] = total + v(site) * values[member]
+                values = fresh
+            for block in range(16):
+                xin[half, block, where, :] = values[block]
+
+    @pl.loop(0, 16)
+    def _(count):
+        step = 15 - count
+        block = partner(me, 2 * step) // 2
+        for half in range(2):
+            view = xin.at[half, block]
+            even = view[pl.ds(0, 256, stride=2), :]
+            odd = view[pl.ds(1, 256, stride=2), :]
+            pair = jnp.concatenate([even, odd], axis=1)
+            lanes = dot3((l_hi[...], l_lo[...]), split(pair), ((1,), (1,)))
+            result = dot3(split(lanes), (a_hi[...], a_lo[...]), ((1,), (0,)))
+            for chunk in range(CHUNKS):
+                for low in range(2):
+                    sbuf[chunk, 2 * block + low, 64 * half : 64 * half + 64, :] = result[
+                        64 * chunk : 64 * chunk + 64, 128 * low : 128 * low + 128
+                    ]
+
+        @pl.when(step > 0)
+        def _():
+            copy_to(0, 2 * step + 1).start()
+            copy_to(0, 2 * step).start()
+
+        @pl.when(step == 0)
+        def _():
+            copy_to(0, 1).start()
+
+    def send_chunk(chunk):
+        @pl.loop(0, DEVICES - 1)
+        def _(count):
+            copy_to(chunk, DEVICES - 1 - count).start()
+
+    send_chunk(1)
+    own = [
+        pltpu.make_async_copy(
+            sbuf.at[chunk, me],
+            rbuf.at[chunk, pl.ds(pl.multiple_of(me * 128, 128), 128)],
+            own_sem.at[chunk],
+        )
+        for chunk in range(CHUNKS)
+    ]
+    for copy in own:
+        copy.start()
+
+    rows = lax.broadcasted_iota(jnp.int32, (256, 128), 0)
+    cols = lax.broadcasted_iota(jnp.int32, (256, 128), 1)
+    e0, e1, e2 = digit(cols, 2), digit(cols, 1), digit(cols, 0)
+    first = hop(0, digit(rows, 3), e0) * bond(0, digit(rows, 0), e0)
+    first = first * hop(1, digit(rows, 2), e1) * bond(1, e0, e1)
+    first = first * hop(2, digit(rows, 1), e2) * bond(2, e1, e2) * bond(3, e2, d3)
+    first = jnp.where(cols < 64, first, 0.0)
+    rows = lax.broadcasted_iota(jnp.int32, (128, 256), 0)
+    cols = lax.broadcasted_iota(jnp.int32, (128, 256), 1)
+    f0, f1, f2 = digit(cols, 2), digit(cols, 1), digit(cols, 0)
+    last = hop(13, digit(rows, 2), f0) * bond(13, digit(cols, 3), f0)
+    last = last * hop(14, digit(rows, 1), f1) * bond(14, f0, f1)
+    last = last * hop(15, digit(rows, 0), f2) * bond(15, f1, f2)
+    both = lax.dot_general(
+        first, last, (((1,), (0,)), ((), ())),
+        precision=lax.Precision.HIGHEST, preferred_element_type=jnp.float32,
+    )
+    rows = lax.broadcasted_iota(jnp.int32, (256, 256), 0)
+    cols = lax.broadcasted_iota(jnp.int32, (256, 256), 1)
+    both = both * hop(12, digit(rows, 0), digit(cols, 3))
+    for d11 in range(4):
+        k_hi[d11], k_lo[d11] = split(both * bond(12, d11, digit(cols, 3)))
+
+    rows = lax.broadcasted_iota(jnp.int32, (64, 128), 0)
+    cols = lax.broadcasted_iota(jnp.int32, (64, 128), 1)
+    d5 = 2 * d5_high + cols // 64
+    table = bond(5, d4, d5) * bond(6, d5, digit(cols, 2)) * bond(7, digit(cols, 2), digit(cols, 1))
+    table = table * bond(8, digit(cols, 1), digit(cols, 0)) * bond(9, digit(cols, 0), digit(rows, 2))
+    table = table * bond(10, digit(rows, 2), digit(rows, 1)) * bond(11, digit(rows, 1), digit(rows, 0))
+    factor[...] = table * bond(4, d3 + 0 * cols, d4)
+    part[...] = jnp.zeros_like(part)
+
+    for copy in own:
+        copy.wait()
+
+    def store_of(chunk):
+        return pltpu.make_async_copy(stage.at[chunk], u_hbm.at[:, chunk], out_sem.at[chunk])
+
+    @pl.loop(0, CHUNKS)
+    def _(chunk):
+        @pl.loop(1, DEVICES)
+        def _(step):
+            copy_to(chunk, step).wait()
+
+        @pl.when(chunk + 2 < CHUNKS)
+        def _():
+            send_chunk(chunk + 2)
+
+        received = rbuf.at[chunk]
+
+        for rest in range(16):
+            values = received[pl.ds(rest, 256, stride=16), :]
+            values = values * factor[pl.ds(chunk * 16 + rest, 1), :]
+            turned = split(values.T)
+            result = dot3(turned, (k_hi[rest % 4], k_lo[rest % 4]), ((1,), (0,)))
+            for high in range(2):
+                piece = result[:, 128 * high : 128 * high + 128]
+                stage[chunk, :, 2 * rest + high, :] = piece
+                part[...] += jnp.sum(piece.reshape(16, 8, 128), axis=0)
+        store_of(chunk).start()
+
+    gathered[pl.ds(me, 1)] = part[...][None]
+
+    def sum_to(step):
+        return pltpu.make_async_remote_copy(
+            src_ref=part,
+            dst_ref=gathered.at[me],
+            send_sem=sum_send.at[step],
+            recv_sem=sum_recv.at[step],
+            device_id=place_of(partner(me, step)),
+            device_id_type=MESH,
+        )
+
+    @pl.loop(1, DEVICES)
+    def _(step):
+        sum_to(step).start()
+
+    @pl.loop(0, CHUNKS)
+    def _(chunk):
+        store_of(chunk).wait()
+
+    @pl.loop(1, DEVICES)
+    def _(step):
+        sum_to(step).wait()
+
+    total_ref[...] = jnp.sum(gathered[...], axis=0)
+
+
+def exchanged(state, couplings):
+    f32, bf16 = jnp.float32, jnp.bfloat16
+    dma = pltpu.SemaphoreType.DMA
+    unscaled, total = pl.pallas_call(
+        exchange_kernel,
+        out_shape=(
+            jax.ShapeDtypeStruct((128, CHUNKS, 32, 128), f32),
+            jax.ShapeDtypeStruct((8, 128), f32),
+        ),
+        in_specs=[pl.BlockSpec(memory_space=pltpu.SMEM), pl.BlockSpec(memory_space=pl.ANY)],
+        out_specs=(pl.BlockSpec(memory_space=pl.ANY), pl.BlockSpec(memory_space=pltpu.VMEM)),
+        scratch_shapes=[
+            pltpu.VMEM((2, 16, 512, 128), f32),
+            pltpu.VMEM((CHUNKS, DEVICES, 128, 128), f32),
+            pltpu.VMEM((CHUNKS, 4096, 128), f32),
+            pltpu.VMEM((CHUNKS, 128, 32, 128), f32),
+            pltpu.VMEM((256, 256), bf16),
+            pltpu.VMEM((256, 256), bf16),
+            pltpu.VMEM((256, 256), bf16),
+            pltpu.VMEM((256, 256), bf16),
+            pltpu.VMEM((4, 256, 256), bf16),
+            pltpu.VMEM((4, 256, 256), bf16),
+            pltpu.VMEM((64, 128), f32),
+            pltpu.VMEM((8, 128), f32),
+            pltpu.VMEM((DEVICES, 8, 128), f32),
+            dma((2,)),
+            dma((CHUNKS,)),
+            dma((CHUNKS,)),
+            dma((CHUNKS, DEVICES)),
+            dma((CHUNKS, DEVICES)),
+            dma((DEVICES,)),
+            dma((DEVICES,)),
+        ],
+        compiler_params=pltpu.CompilerParams(
+            collective_id=0, has_side_effects=True, vmem_limit_bytes=48 * 2**20
+        ),
+    )(couplings, state.reshape(2, 16, 512, 128))
+    mean_value = jnp.sum(total) / (state.shape[0] * DEVICES)
+    return unscaled.reshape(-1) * (1.0 / mean_value), jnp.log(mean_value)
+
+
 def solution(mesh):
     in_specs = (P(("lead", "sub")), P())
     out_specs = (P(("lead", "sub")), P())
-    return jax.shard_map(shards, mesh=mesh, in_specs=in_specs, out_specs=out_specs, check_vma=False)
+    body = exchanged if dict(mesh.shape) == {"lead": 8, "sub": 4} else shards
+    return jax.shard_map(body, mesh=mesh, in_specs=in_specs, out_specs=out_specs, check_vma=False)

time: 794 us -> 224 us (0.28); the launches traced: 779 us -> 224 us
  waiting for transfers between devices: 336 us -> 0 us
  local copies, waits for them, and re-layouts: 240 us -> 0.67 us
  Pallas kernels: 0 us -> 212 us
  blocking collectives: 83.1 us -> 0 us
  matrix products: 65.9 us -> 0 us
  other arithmetic: 37.9 us -> 9.34 us
  starting transfers between devices: 13.2 us -> 0 us
    all_to_all x2 -> x0, waiting for transfers between devices: 336 us -> none  [regroup(): lax.all_to_all(shaped, ('lead', 'sub'), split_axis=2, concat_axis=0, tile...]
    pallas_call x0 -> x1, Pallas kernels: none -> 212 us  [exchanged(): pl.pallas_call(exchange_kernel, out_shape=(jax.ShapeDtypeStruct((128, CHU...]
    psum x2 -> x0, blocking collectives: 83.1 us -> none  [shards(): grand_total = lax.psum(jnp.sum(current), ('lead', 'sub'))]
    reshape x5 -> x0, local copies, waits for them, and re-layouts: 70.1 us -> none  [the longest x2 42.4 us: regroup(): shaped = current.reshape(1, low_rows, devices, rest_cols)]
    dot_general x4 -> x0, matrix products: 65.9 us -> none  [multiply(): lax.dot_general(matrix, kernel, (((0,), (0,)), ((), ())), precision=lax.P...]
    dot_general x6 -> x0, local copies, waits for them, and re-layouts: 57.5 us -> none  [multiply(): lax.dot_general(matrix, kernel, (((0,), (0,)), ((), ())), precision=lax.P...]
    mul x3 -> x0, local copies, waits for them, and re-layouts: 39 us -> none  [bond_first(): result.reshape(-1, 4, 4, spread // 4) * first_bond[None, :, :, None]]
    div x2 -> x0, local copies, waits for them, and re-layouts: 31.4 us -> none  [shards(): current = current / mean_value]
  transfers between devices with their start and end apart: 2 -> 0, of which waited for: 2 -> 0; matrix products, arithmetic and copies ran while one was open for 4% -> 0% of each run, Pallas kernels for 0% -> 0%
where the time goes in v1:
time: 224 us
  Pallas kernels  212 us (95%)
  other arithmetic  9.34 us (4%)
  between operations  2.51 us (1%)
    pallas_call x1, Pallas kernels, exchanged(): pl.pallas_call(exchange_kernel, out_shape=(jax.ShapeDtypeStruct((128, CHU...  212 us
    mul x1, other arithmetic, exchanged(): return (unscaled.reshape(-1) * (1.0 / mean_value), jnp.log(mean_value))  8.74 us

profile of v1, /device:TPU:0, one launch (start us, length us, event | category | flops | bytes accessed | tf_op | source)
XLA Modules:
  0.0 224.2 jit_solution(5196322619458010714)
XLA Ops:
  0.6 0.0 copy-start
  0.6 0.7 copy-done
  1.3 211.7 %shard_map.41 = (f32[128,4,32,128]{3,2,1,0:T(8,128)}, f32[8,128]{1,0:T(8,128)S(1)}) custom-call(f32[2,16]{1,0:T(2,128)S(1)} %copy-done, f32[2,16,512,128]{3,2,1,0:T(8,128)} %bitcast.3), custom_call_target="tpu_custom_call" | custom-call | tf_op jit(solution)/shard_map/pallas_call | solution.py:342
  213.0 0.6 reduce_sum.9
  214.3 8.7 %broadcast_multiply_fusion = f32[128,4,32,128]{3,2,1,0:T(8,128)} fusion(f32[128,4,32,128]{3,2,1,0:T(8,128)} %get-tuple-element.4, f32[]{:T(128)S(6)} %div.7), kind=kLoop, calls=%fused_computation | loop fusion | flops 2097152 | bytes 16777220 | tf_op jit(solution)/shard_map/mul | solution.py:377
Async XLA Ops:
  0.6 0.7 copy-start

commit v2 on v1

--- a/solution.py
+++ b/solution.py
@@ -126,9 +126,9 @@
 
 
 def exchange_kernel(
-    coup, x_hbm, u_hbm, total_ref,
-    xin, sbuf, rbuf, stage, l_hi, l_lo, a_hi, a_lo, k_hi, k_lo, factor, part, gathered,
-    in_sem, out_sem, own_sem, send_sem, recv_sem, sum_send, sum_recv,
+    coup, x_hbm, u_ref, total_ref,
+    xin, sbuf, rbuf, l_hi, l_lo, a_hi, a_lo, k_hi, k_lo, factor, part, gathered,
+    in_sem, own_sem, send_sem, recv_sem, sum_send, sum_recv,
 ):
     me = lax.axis_index("lead") * 4 + lax.axis_index("sub")
     d3, d4, d5_high = me // 8, (me // 2) % 4, me % 2
@@ -152,8 +152,6 @@
         pl.semaphore_signal(
             barrier, inc=1, device_id=place_of(partner(me, step)), device_id_type=MESH
         )
-
-    pl.semaphore_wait(barrier, DEVICES - 1)
 
     def bond(site, one, other):
         return jnp.where(one == other, 1.0 + h(site), 1.0)
@@ -205,9 +203,11 @@
             for block in range(16):
                 xin[half, block, where, :] = values[block]
 
+    pl.semaphore_wait(barrier, DEVICES - 1)
+
     @pl.loop(0, 16)
     def _(count):
-        step = 15 - count
+        step = 15 - count // 2 - 8 * (count % 2)
         block = partner(me, 2 * step) // 2
         for half in range(2):
             view = xin.at[half, block]
@@ -234,7 +234,7 @@
     def send_chunk(chunk):
         @pl.loop(0, DEVICES - 1)
         def _(count):
-            copy_to(chunk, DEVICES - 1 - count).start()
+            copy_to(chunk, DEVICES - 1 - count // 2 - 16 * (count % 2)).start()
 
     send_chunk(1)
     own = [
@@ -283,9 +283,6 @@
     for copy in own:
         copy.wait()
 
-    def store_of(chunk):
-        return pltpu.make_async_copy(stage.at[chunk], u_hbm.at[:, chunk], out_sem.at[chunk])
-
     @pl.loop(0, CHUNKS)
     def _(chunk):
         @pl.loop(1, DEVICES)
@@ -298,16 +295,23 @@
 
         received = rbuf.at[chunk]
 
-        for rest in range(16):
-            values = received[pl.ds(rest, 256, stride=16), :]
-            values = values * factor[pl.ds(chunk * 16 + rest, 1), :]
-            turned = split(values.T)
-            result = dot3(turned, (k_hi[rest % 4], k_lo[rest % 4]), ((1,), (0,)))
-            for high in range(2):
-                piece = result[:, 128 * high : 128 * high + 128]
-                stage[chunk, :, 2 * rest + high, :] = piece
-                part[...] += jnp.sum(piece.reshape(16, 8, 128), axis=0)
-        store_of(chunk).start()
+        for d11 in range(4):
+            turned = []
+            for d10 in range(4):
+                rest = 4 * d10 + d11
+                values = received[pl.ds(rest, 256, stride=16), :]
+                values = values * factor[pl.ds(chunk * 16 + rest, 1), :]
+                turned.append(values.T)
+            turned = split(jnp.concatenate(turned, axis=0))
+            result = dot3(turned, (k_hi[d11], k_lo[d11]), ((1,), (0,)))
+            part[...] += jnp.sum(
+                (result[:, :128] + result[:, 128:]).reshape(64, 8, 128), axis=0
+            )
+            for d10 in range(4):
+                for high in range(2):
+                    u_ref[:, chunk, 8 * d10 + 2 * d11 + high, :] = result[
+                        128 * d10 : 128 * d10 + 128, 128 * high : 128 * high + 128
+                    ]
 
     gathered[pl.ds(me, 1)] = part[...][None]
 
@@ -324,10 +328,6 @@
     @pl.loop(1, DEVICES)
     def _(step):
         sum_to(step).start()
-
-    @pl.loop(0, CHUNKS)
-    def _(chunk):
-        store_of(chunk).wait()
 
     @pl.loop(1, DEVICES)
     def _(step):
@@ -346,12 +346,11 @@
             jax.ShapeDtypeStruct((8, 128), f32),
         ),
         in_specs=[pl.BlockSpec(memory_space=pltpu.SMEM), pl.BlockSpec(memory_space=pl.ANY)],
-        out_specs=(pl.BlockSpec(memory_space=pl.ANY), pl.BlockSpec(memory_space=pltpu.VMEM)),
+        out_specs=(pl.BlockSpec(memory_space=pltpu.VMEM),) * 2,
         scratch_shapes=[
             pltpu.VMEM((2, 16, 512, 128), f32),
             pltpu.VMEM((CHUNKS, DEVICES, 128, 128), f32),
             pltpu.VMEM((CHUNKS, 4096, 128), f32),
-            pltpu.VMEM((CHUNKS, 128, 32, 128), f32),
             pltpu.VMEM((256, 256), bf16),
             pltpu.VMEM((256, 256), bf16),
             pltpu.VMEM((256, 256), bf16),
@@ -363,14 +362,13 @@
             pltpu.VMEM((DEVICES, 8, 128), f32),
             dma((2,)),
             dma((CHUNKS,)),
-            dma((CHUNKS,)),
             dma((CHUNKS, DEVICES)),
             dma((CHUNKS, DEVICES)),
             dma((DEVICES,)),
             dma((DEVICES,)),
         ],
         compiler_params=pltpu.CompilerParams(
-            collective_id=0, has_side_effects=True, vmem_limit_bytes=48 * 2**20
+            collective_id=0, has_side_effects=True, vmem_limit_bytes=40 * 2**20
         ),
     )(couplings, state.reshape(2, 16, 512, 128))
     mean_value = jnp.sum(total) / (state.shape[0] * DEVICES)

time: 224 us -> 224 us (level)
  Pallas kernels: 212 us -> 207 us
  local copies, waits for them, and re-layouts: 0.67 us -> 4.06 us
    pallas_call x1, Pallas kernels: 212 us -> 207 us  [exchanged(): pl.pallas_call(exchange_kernel, out_shape=(jax.ShapeDtypeStruct((128, CHU...]
    unnamed x2 -> x4, local copies, waits for them, and re-layouts: 0.67 us -> 4.06 us
where the time goes in v2:
time: 224 us; the launch traced here: 223 us
  Pallas kernels  207 us (92%)
  other arithmetic  9.34 us (4%)
  local copies, waits for them, and re-layouts  4.06 us (2%)
  between operations  2.52 us (1%)
    pallas_call x1, Pallas kernels, exchanged(): pl.pallas_call(exchange_kernel, out_shape=(jax.ShapeDtypeStruct((128, CHU...  207 us
    mul x1, other arithmetic, exchanged(): return (unscaled.reshape(-1) * (1.0 / mean_value), jnp.log(mean_value))  8.74 us

profile of v2, /device:TPU:0, one launch (start us, length us, event | category | flops | bytes accessed | tf_op | source)
XLA Modules:
  0.0 223.4 jit_solution(11988163923972128832)
XLA Ops:
  0.6 0.0 copy-start.1
  0.6 0.7 copy-done.1
  1.3 207.5 %shard_map.41 = (f32[128,4,32,128]{3,2,1,0:T(8,128)S(1)}, f32[8,128]{1,0:T(8,128)S(1)}) custom-call(f32[2,16]{1,0:T(2,128)S(1)} %copy-done.1, f32[2,16,512,128]{3,2,1,0:T(8,128)} %bitcast.3), custom_call_target="tpu_custom_call" | custom-call | tf_op jit(solution)/shard_map/pallas_call | solution.py:342
  208.8 0.0 copy-start
  208.8 3.4 %copy-done = f32[128,4,32,128]{3,2,1,0:T(8,128)} copy-done((f32[128,4,32,128]{3,2,1,0:T(8,128)}, f32[128,4,32,128]{3,2,1,0:T(8,128)S(1)}, u32[]{:S(2)}) %copy-start) | copy-done | bytes 8388632
  212.2 0.6 reduce_sum.9
  213.5 8.7 %broadcast_multiply_fusion = f32[128,4,32,128]{3,2,1,0:T(8,128)} fusion(f32[128,4,32,128]{3,2,1,0:T(8,128)} %copy-done, f32[]{:T(128)S(6)} %div.7), kind=kLoop, calls=%fused_computation | loop fusion | flops 2097152 | bytes 16777220 | tf_op jit(solution)/shard_map/mul | solution.py:375
Async XLA Ops:
  0.6 0.7 copy-start.1
  208.8 3.4 %copy-start = (f32[128,4,32,128]{3,2,1,0:T(8,128)}, f32[128,4,32,128]{3,2,1,0:T(8,128)S(1)}, u32[]{:S(2)}) copy-start(f32[128,4,32,128]{3,2,1,0:T(8,128)S(1)} %get-tuple-element.4) | copy-start | bytes 25165828

commit v3 on v2

--- a/solution.py
+++ b/solution.py
@@ -1,3 +1,5 @@
+import functools
+
 import jax
 import jax.numpy as jnp
 from jax import lax
@@ -96,6 +98,7 @@
 MESH = pl.DeviceIdType.MESH
 DEVICES = 32
 CHUNKS = 4
+PARTS = 16
 
 
 def split(value):
@@ -236,7 +239,8 @@
         def _(count):
             copy_to(chunk, DEVICES - 1 - count // 2 - 16 * (count % 2)).start()
 
-    send_chunk(1)
+    for chunk in range(1, CHUNKS):
+        send_chunk(chunk)
     own = [
         pltpu.make_async_copy(
             sbuf.at[chunk, me],
@@ -289,10 +293,6 @@
         def _(step):
             copy_to(chunk, step).wait()
 
-        @pl.when(chunk + 2 < CHUNKS)
-        def _():
-            send_chunk(chunk + 2)
-
         received = rbuf.at[chunk]
 
         for d11 in range(4):
@@ -334,6 +334,24 @@
         sum_to(step).wait()
 
     total_ref[...] = jnp.sum(gathered[...], axis=0)
+
+
+def scale_kernel(whole_count, u_ref, total_ref, out_hbm, growth_ref, stage, sem):
+    mean_value = jnp.sum(total_ref[...], keepdims=True) / whole_count
+    growth_ref[...] = jnp.log(mean_value)
+    scale = 1.0 / mean_value
+
+    def store_of(part):
+        return pltpu.make_async_copy(stage.at[part], out_hbm.at[part], sem.at[part])
+
+    @pl.loop(0, PARTS)
+    def _(part):
+        stage[part] = u_ref[part] * scale
+        store_of(part).start()
+
+    @pl.loop(0, PARTS)
+    def _(part):
+        store_of(part).wait()
 
 
 def exchanged(state, couplings):
@@ -371,8 +389,19 @@
             collective_id=0, has_side_effects=True, vmem_limit_bytes=40 * 2**20
         ),
     )(couplings, state.reshape(2, 16, 512, 128))
-    mean_value = jnp.sum(total) / (state.shape[0] * DEVICES)
-    return unscaled.reshape(-1) * (1.0 / mean_value), jnp.log(mean_value)
+    rows = state.shape[0] // (128 * PARTS)
+    evolved, growth = pl.pallas_call(
+        functools.partial(scale_kernel, state.shape[0] * DEVICES),
+        out_shape=(
+            jax.ShapeDtypeStruct((PARTS, rows, 128), f32),
+            jax.ShapeDtypeStruct((1, 1), f32),
+        ),
+        in_specs=[pl.BlockSpec(memory_space=pltpu.VMEM)] * 2,
+        out_specs=(pl.BlockSpec(memory_space=pl.ANY), pl.BlockSpec(memory_space=pltpu.VMEM)),
+        scratch_shapes=[pltpu.VMEM((PARTS, rows, 128), f32), dma((PARTS,))],
+        compiler_params=pltpu.CompilerParams(vmem_limit_bytes=24 * 2**20),
+    )(unscaled.reshape(PARTS, rows, 128), total)
+    return evolved.reshape(-1), growth.reshape(())
 
 
 def solution(mesh):

time: 224 us -> 219 us (0.978)
  Pallas kernels: 207 us -> 217 us
  other arithmetic: 9.34 us -> 0 us
  local copies, waits for them, and re-layouts: 4.06 us -> 0.67 us
    mul x1 -> x0, other arithmetic: 8.74 us -> none  [exchanged(): return (unscaled.reshape(-1) * (1.0 / mean_value), jnp.log(mean_value))]
    pallas_call x1, Pallas kernels: 207 us -> 213 us  [exchanged(): pl.pallas_call(exchange_kernel, out_shape=(jax.ShapeDtypeStruct((128, CHU...]
    pallas_call x0 -> x1, Pallas kernels: none -> 4.08 us  [exchanged(): pl.pallas_call(functools.partial(scale_kernel, state.shape[0] * DEVICES),...]
    unnamed x4 -> x2, local copies, waits for them, and re-layouts: 4.06 us -> 0.67 us
where the time goes in v3:
time: 219 us; the launch traced here: 218 us
  Pallas kernels  217 us (99%)
    pallas_call x1, Pallas kernels, exchanged(): pl.pallas_call(exchange_kernel, out_shape=(jax.ShapeDtypeStruct((128, CHU...  213 us

profile of v3, /device:TPU:0, one launch (start us, length us, event | category | flops | bytes accessed | tf_op | source)
XLA Modules:
  0.0 218.4 jit_solution(2035353476603948515)
XLA Ops:
  0.6 0.0 copy-start
  0.6 0.7 copy-done
  1.3 213.0 %shard_map.41 = (f32[128,4,32,128]{3,2,1,0:T(8,128)S(1)}, f32[8,128]{1,0:T(8,128)S(1)}) custom-call(f32[2,16]{1,0:T(2,128)S(1)} %copy-done, f32[2,16,512,128]{3,2,1,0:T(8,128)} %bitcast.5), custom_call_target="tpu_custom_call" | custom-call | tf_op jit(solution)/shard_map/pallas_call | solution.py:360
  214.3 4.1 %shard_map.42 = (f32[16,1024,128]{2,1,0:T(8,128)}, f32[1,1]{1,0:T(1,128)}) custom-call(f32[16,1024,128]{2,1,0:T(8,128)S(1)} %bitcast.4, f32[8,128]{1,0:T(8,128)S(1)} %get-tuple-element.7.total_ref), custom_call_target="tpu_custom_call" | custom-call | tf_op jit(solution)/shard_map/pallas_call | solution.py:393
Async XLA Ops:
  0.6 0.7 copy-start

commit v4 on v3

--- a/solution.py
+++ b/solution.py
@@ -116,9 +116,9 @@
     return (index // 4**place) % 4
 
 
-def partner(me, step):
+def partner(me, step, bits=5):
     other = 0
-    for bit in range(5):
+    for bit in range(bits):
         a, b = (me // 2**bit) % 2, (step // 2**bit) % 2
         other = other + (a + b - 2 * a * b) * 2**bit
     return other
@@ -130,11 +130,12 @@
 
 def exchange_kernel(
     coup, x_hbm, u_ref, total_ref,
-    xin, sbuf, rbuf, l_hi, l_lo, a_hi, a_lo, k_hi, k_lo, factor, part, gathered,
-    in_sem, own_sem, send_sem, recv_sem, sum_send, sum_recv,
+    xin, sbuf, abuf, rbuf, l_hi, l_lo, a_hi, a_lo, k_hi, k_lo, factor, part, gathered,
+    in_sem, own_sem, a_send, a_recv, b_send, b_recv, sum_send, sum_recv,
 ):
     me = lax.axis_index("lead") * 4 + lax.axis_index("sub")
     d3, d4, d5_high = me // 8, (me // 2) % 4, me % 2
+    plane, spot = me // 8, me % 8
 
     def v(site):
         return coup[0, site]
@@ -172,16 +173,83 @@
     l_mat = jnp.where(digit(rows, 2) == digit(cols, 0), l_mat, 0.0)
     l_hi[...], l_lo[...] = split(l_mat)
 
-    def copy_to(chunk, step):
-        other = partner(me, step)
+    def received_from(source):
+        return pl.ds(pl.multiple_of(source * 128, 128), 128)
+
+    def within(chunk, turn, hop):
+        there, target = partner(spot, hop, 3), partner(plane, turn, 2)
         return pltpu.make_async_remote_copy(
-            src_ref=sbuf.at[chunk, other],
-            dst_ref=rbuf.at[chunk, pl.ds(pl.multiple_of(me * 128, 128), 128)],
-            send_sem=send_sem.at[chunk, step],
-            recv_sem=recv_sem.at[chunk, step],
-            device_id=place_of(other),
+            src_ref=sbuf.at[chunk, 8 * target + there],
+            dst_ref=abuf.at[chunk, turn, spot],
+            send_sem=a_send.at[chunk, turn, hop],
+            recv_sem=a_recv.at[chunk, turn, hop],
+            device_id=place_of(8 * plane + there),
             device_id_type=MESH,
         )
+
+    def settle(chunk, hop):
+        there = partner(spot, hop, 3)
+        return pltpu.make_async_remote_copy(
+            src_ref=sbuf.at[chunk, 8 * plane + there],
+            dst_ref=rbuf.at[chunk, received_from(me)],
+            send_sem=a_send.at[chunk, 0, hop],
+            recv_sem=a_recv.at[chunk, 0, hop],
+            device_id=place_of(8 * plane + there),
+            device_id_type=MESH,
+        )
+
+    def across(chunk, turn, hop, source=None):
+        origin, target = partner(spot, hop, 3), partner(plane, turn, 2)
+        return pltpu.make_async_remote_copy(
+            src_ref=abuf.at[chunk, turn, origin] if source is None else source,
+            dst_ref=rbuf.at[chunk, received_from(8 * plane + origin)],
+            send_sem=b_send.at[chunk, turn, hop],
+            recv_sem=b_recv.at[chunk, turn, hop],
+            device_id=place_of(8 * target + spot),
+            device_id_type=MESH,
+        )
+
+    def across_own(chunk, turn):
+        target = partner(plane, turn, 2)
+        return across(chunk, turn, 0, sbuf.at[chunk, 8 * target + spot])
+
+    def depart(chunk, count):
+        turn, half = 3 - count // 4, 3 - count % 4
+
+        @pl.when(turn > 0)
+        def _():
+            within(chunk, turn, 2 * half + 1).start()
+
+            @pl.when(half > 0)
+            def _():
+                within(chunk, turn, 2 * half).start()
+
+            @pl.when(half == 0)
+            def _():
+                across_own(chunk, turn).start()
+
+        @pl.when(turn == 0)
+        def _():
+            settle(chunk, 2 * half + 1).start()
+
+            @pl.when(half > 0)
+            def _():
+                settle(chunk, 2 * half).start()
+
+    def depart_all(chunk):
+        @pl.loop(0, 16)
+        def _(count):
+            depart(chunk, count)
+
+    def forward(chunk):
+        @pl.loop(0, 3)
+        def _(count):
+            turn = 3 - count
+
+            @pl.loop(1, 8)
+            def _(hop):
+                within(chunk, turn, 8 - hop).wait_recv()
+                across(chunk, turn, 8 - hop).start()
 
     for load in loads:
         load.wait()
@@ -210,8 +278,7 @@
 
     @pl.loop(0, 16)
     def _(count):
-        step = 15 - count // 2 - 8 * (count % 2)
-        block = partner(me, 2 * step) // 2
+        block = partner(me // 2, 15 - count, 4)
         for half in range(2):
             view = xin.at[half, block]
             even = view[pl.ds(0, 256, stride=2), :]
@@ -225,22 +292,11 @@
                         64 * chunk : 64 * chunk + 64, 128 * low : 128 * low + 128
                     ]
 
-        @pl.when(step > 0)
-        def _():
-            copy_to(0, 2 * step + 1).start()
-            copy_to(0, 2 * step).start()
-
-        @pl.when(step == 0)
-        def _():
-            copy_to(0, 1).start()
-
-    def send_chunk(chunk):
-        @pl.loop(0, DEVICES - 1)
-        def _(count):
-            copy_to(chunk, DEVICES - 1 - count // 2 - 16 * (count % 2)).start()
-
-    for chunk in range(1, CHUNKS):
-        send_chunk(chunk)
+        depart(0, count)
+
+    depart_all(1)
+    forward(0)
+    depart_all(2)
     own = [
         pltpu.make_async_copy(
             sbuf.at[chunk, me],
@@ -287,11 +343,26 @@
     for copy in own:
         copy.wait()
 
+    forward(1)
+    depart_all(3)
+    forward(2)
+    forward(3)
+
     @pl.loop(0, CHUNKS)
     def _(chunk):
-        @pl.loop(1, DEVICES)
-        def _(step):
-            copy_to(chunk, step).wait()
+        @pl.loop(1, 8)
+        def _(hop):
+            settle(chunk, hop).wait()
+
+        @pl.loop(0, 3)
+        def _(count):
+            @pl.loop(0, 8)
+            def _(hop):
+                across(chunk, 3 - count, hop).wait()
+
+            @pl.loop(1, 8)
+            def _(hop):
+                within(chunk, 3 - count, hop).wait_send()
 
         received = rbuf.at[chunk]
 
@@ -368,6 +439,7 @@
         scratch_shapes=[
             pltpu.VMEM((2, 16, 512, 128), f32),
             pltpu.VMEM((CHUNKS, DEVICES, 128, 128), f32),
+            pltpu.VMEM((CHUNKS, 4, 8, 128, 128), f32),
             pltpu.VMEM((CHUNKS, 4096, 128), f32),
             pltpu.VMEM((256, 256), bf16),
             pltpu.VMEM((256, 256), bf16),
@@ -380,13 +452,15 @@
             pltpu.VMEM((DEVICES, 8, 128), f32),
             dma((2,)),
             dma((CHUNKS,)),
-            dma((CHUNKS, DEVICES)),
-            dma((CHUNKS, DEVICES)),
+            dma((CHUNKS, 4, 8)),
+            dma((CHUNKS, 4, 8)),
+            dma((CHUNKS, 4, 8)),
+            dma((CHUNKS, 4, 8)),
             dma((DEVICES,)),
             dma((DEVICES,)),
         ],
         compiler_params=pltpu.CompilerParams(
-            collective_id=0, has_side_effects=True, vmem_limit_bytes=40 * 2**20
+            collective_id=0, has_side_effects=True, vmem_limit_bytes=44 * 2**20
         ),
     )(couplings, state.reshape(2, 16, 512, 128))
     rows = state.shape[0] // (128 * PARTS)

time: 219 us -> 226 us (1.032)
  Pallas kernels: 217 us -> 225 us
    pallas_call x1, Pallas kernels: 213 us -> 221 us  [exchanged(): pl.pallas_call(exchange_kernel, out_shape=(jax.ShapeDtypeStruct((128, CHU...]
where the time goes in v4:
time: 226 us
  Pallas kernels  225 us (100%)
    pallas_call x1, Pallas kernels, exchanged(): pl.pallas_call(exchange_kernel, out_shape=(jax.ShapeDtypeStruct((128, CHU...  221 us

profile of v4, /device:TPU:0, one launch (start us, length us, event | category | flops | bytes accessed | tf_op | source)
XLA Modules:
  0.0 226.2 jit_solution(4407173341642022013)
XLA Ops:
  0.6 0.0 copy-start
  0.6 0.7 copy-done
  1.3 220.8 %shard_map.41 = (f32[128,4,32,128]{3,2,1,0:T(8,128)S(1)}, f32[8,128]{1,0:T(8,128)S(1)}) custom-call(f32[2,16]{1,0:T(2,128)S(1)} %copy-done, f32[2,16,512,128]{3,2,1,0:T(8,128)} %bitcast.5), custom_call_target="tpu_custom_call" | custom-call | tf_op jit(solution)/shard_map/pallas_call | solution.py:431
  222.2 4.1 %shard_map.42 = (f32[16,1024,128]{2,1,0:T(8,128)}, f32[1,1]{1,0:T(1,128)}) custom-call(f32[16,1024,128]{2,1,0:T(8,128)S(1)} %bitcast.4, f32[8,128]{1,0:T(8,128)S(1)} %get-tuple-element.7.total_ref), custom_call_target="tpu_custom_call" | custom-call | tf_op jit(solution)/shard_map/pallas_call | solution.py:467
Async XLA Ops:
  0.6 0.7 copy-start

commit v5 on v3

--- a/solution.py
+++ b/solution.py
@@ -99,6 +99,7 @@
 DEVICES = 32
 CHUNKS = 4
 PARTS = 16
+WINDOW = 16
 
 
 def split(value):
@@ -234,13 +235,16 @@
         def _():
             copy_to(0, 1).start()
 
+    def numbered(number):
+        count = number % (DEVICES - 1)
+        return copy_to(number // (DEVICES - 1), DEVICES - 1 - count // 2 - 16 * (count % 2))
+
     def send_chunk(chunk):
-        @pl.loop(0, DEVICES - 1)
-        def _(count):
-            copy_to(chunk, DEVICES - 1 - count // 2 - 16 * (count % 2)).start()
-
-    for chunk in range(1, CHUNKS):
-        send_chunk(chunk)
+        @pl.loop(chunk * (DEVICES - 1), (chunk + 1) * (DEVICES - 1))
+        def _(number):
+            numbered(number - WINDOW).wait_send()
+            numbered(number).start()
+
     own = [
         pltpu.make_async_copy(
             sbuf.at[chunk, me],
@@ -287,11 +291,18 @@
     for copy in own:
         copy.wait()
 
+    @pl.loop(0, DEVICES - 1 - WINDOW)
+    def _(number):
+        numbered(number).wait_send()
+
+    send_chunk(1)
+    send_chunk(2)
+
     @pl.loop(0, CHUNKS)
     def _(chunk):
         @pl.loop(1, DEVICES)
         def _(step):
-            copy_to(chunk, step).wait()
+            copy_to(chunk, step).wait_recv()
 
         received = rbuf.at[chunk]
 
@@ -312,6 +323,14 @@
                     u_ref[:, chunk, 8 * d10 + 2 * d11 + high, :] = result[
                         128 * d10 : 128 * d10 + 128, 128 * high : 128 * high + 128
                     ]
+
+        @pl.when(chunk == 0)
+        def _():
+            send_chunk(3)
+
+    @pl.loop(CHUNKS * (DEVICES - 1) - WINDOW, CHUNKS * (DEVICES - 1))
+    def _(number):
+        numbered(number).wait_send()
 
     gathered[pl.ds(me, 1)] = part[...][None]
 

time: 219 us -> 217 us (level)
  no operation moved by 1% of the time
where the time goes in v5:
time: 217 us
  Pallas kernels  216 us (100%)
    pallas_call x1, Pallas kernels, exchanged(): pl.pallas_call(exchange_kernel, out_shape=(jax.ShapeDtypeStruct((128, CHU...  212 us

profile of v5, /device:TPU:0, one launch (start us, length us, event | category | flops | bytes accessed | tf_op | source)
XLA Modules:
  0.0 217.2 jit_solution(13570314058706679528)
XLA Ops:
  0.6 0.0 copy-start
  0.6 0.7 copy-done
  1.3 211.8 %shard_map.41 = (f32[128,4,32,128]{3,2,1,0:T(8,128)S(1)}, f32[8,128]{1,0:T(8,128)S(1)}) custom-call(f32[2,16]{1,0:T(2,128)S(1)} %copy-done, f32[2,16,512,128]{3,2,1,0:T(8,128)} %bitcast.5), custom_call_target="tpu_custom_call" | custom-call | tf_op jit(solution)/shard_map/pallas_call | solution.py:379
  213.1 4.1 %shard_map.42 = (f32[16,1024,128]{2,1,0:T(8,128)}, f32[1,1]{1,0:T(1,128)}) custom-call(f32[16,1024,128]{2,1,0:T(8,128)S(1)} %bitcast.4, f32[8,128]{1,0:T(8,128)S(1)} %get-tuple-element.7.total_ref), custom_call_target="tpu_custom_call" | custom-call | tf_op jit(solution)/shard_map/pallas_call | solution.py:412
Async XLA Ops:
  0.6 0.7 copy-start
